TPU v7x, 32 devices: a whole 2x2x4 slice. The times are simulated.
32 devices in a mesh: dp: 4 (over z), expert: 4 (over y, core), tensor: 2 (over x).
Axes of the slice: x: 2, y: 2, z: 4, core: 2. Of those that a mesh axis runs over, the one named last changes fastest.
Arguments:
- grad_out: bfloat16 [2048, 4096], P(('dp', 'expert'), 'tensor'), may hold values from -2 to 2
- route_ids: int32 [2048, 2], P(('dp', 'expert')), may hold values from 0 to 3, all different within a row; in each aligned block of 128 rows (0 to 127, 128 to 255, ...) at most 80 rows name the same one
- route_probs: bfloat16 [2048, 2], P(('dp', 'expert')), may hold values from 0.19921875 to 1
- saved_pre: bfloat16 [4, 4, 320, 1536], P('dp', 'expert'), may hold values from -6 to 6
- w_gate: bfloat16 [4, 4096, 768], P('expert', 'tensor'), may hold values from -0.21875 to 0.21875
- w_up: bfloat16 [4, 4096, 768], P('expert', 'tensor'), may hold values from -0.21875 to 0.21875
- w_down: bfloat16 [4, 768, 4096], P('expert', None, 'tensor'), may hold values from -0.09375 to 0.09375
Outputs:
- token_grad: bfloat16 [2048, 4096], P(('dp', 'expert'), 'tensor')
- prob_grad: bfloat16 [2048, 2], P(('dp', 'expert'))
- grad_down: bfloat16 [4, 768, 4096], P('expert', 'dp', 'tensor')
Inputs may be any that keep to these rules, and one draw needn't show every extreme that they name: `route_ids`: each row names 2 different experts. In each aligned block of 128 rows (the tokens of one device) no expert is named by more than 80 rows, a bound that some block reaches.
All inputs are finite; a program needn't handle non-finite values.
Results may differ from a plain program's by a relative error of at most 0.015.
Values may be sent and summed in bfloat16 or wider, within the bound.
A program may use at most 64 MiB of HBM per device.

v0:
```python
import jax
import jax.numpy as jnp
from jax import lax
from jax.sharding import PartitionSpec as P


def slot_index(id_block, n_experts, capacity):
    flat = id_block.reshape(-1)
    onehot = (flat[:, None] == jnp.arange(n_experts, dtype=jnp.int32)[None, :]).astype(jnp.int32)
    before = jnp.cumsum(onehot, axis=0) - onehot
    position = jnp.sum(before * onehot, axis=1)
    return flat * capacity + position


def backward_rows(dh_rows, gate, upper, sig, act, hid, p32):
    route = jnp.sum(dh_rows * hid, axis=1).astype(jnp.bfloat16)
    scaled = p32 * dh_rows
    dgate = (scaled * upper * sig * (1.0 + gate * (1.0 - sig))).astype(jnp.bfloat16)
    dup = (scaled * act).astype(jnp.bfloat16)
    return (dgate, dup, route)


def shards(grad_out, route_ids, route_probs, saved_pre, w_gate, w_up, w_down):
    n_exp = lax.axis_size("expert")
    slot_rows = saved_pre.shape[2]
    capacity = slot_rows // n_exp
    tok = grad_out.shape[0]
    topk = route_ids.shape[1]
    width = grad_out.shape[1]
    hidden = saved_pre.shape[3] // 2
    slots = slot_index(route_ids, n_exp, capacity)
    source = (
        jnp.zeros((n_exp * capacity,), jnp.int32)
        .at[slots]
        .set(jnp.arange(tok * topk, dtype=jnp.int32) + 1)
    )
    valid = source > 0
    flat_src = jnp.maximum(source - 1, 0)
    send_rows = jnp.where(valid[:, None], grad_out[flat_src // topk], jnp.zeros((), jnp.bfloat16))
    send_prob = jnp.where(valid, route_probs.reshape(-1)[flat_src], jnp.zeros((), jnp.bfloat16))
    got_rows, got_prob = (
        lax.all_to_all(
            send_rows.reshape(n_exp, capacity, width),
            "expert",
            split_axis=0,
            concat_axis=0,
            tiled=True,
        ),
        lax.all_to_all(
            send_prob.reshape(n_exp, capacity), "expert", split_axis=0, concat_axis=0, tiled=True
        ),
    )
    dyr = got_rows.reshape(slot_rows, width)
    p32 = got_prob.reshape(slot_rows, 1).astype(jnp.float32)
    pre = saved_pre[0, 0]
    gate = pre[:, :hidden].astype(jnp.float32)
    upper = pre[:, hidden:].astype(jnp.float32)
    sig = jax.nn.sigmoid(gate)
    act = gate * sig
    hid = act * upper
    hpro = (p32 * hid).astype(jnp.bfloat16)
    down_term = lax.dot_general(
        hpro, dyr, (((0,), (0,)), ((), ())), preferred_element_type=jnp.float32
    )
    dh_part = lax.dot_general(
        dyr, w_down[0], (((1,), (1,)), ((), ())), preferred_element_type=jnp.float32
    )
    dh_rows = lax.psum(dh_part.astype(jnp.bfloat16), "tensor").astype(jnp.float32)
    dgate, dup, route = backward_rows(dh_rows, gate, upper, sig, act, hid, p32)
    dx = lax.dot_general(
        dgate, w_gate[0], (((1,), (1,)), ((), ())), preferred_element_type=jnp.float32
    )
    dx = dx + lax.dot_general(
        dup, w_up[0], (((1,), (1,)), ((), ())), preferred_element_type=jnp.float32
    )
    dx = dx.astype(jnp.bfloat16)
    back_rows, back_route = (
        lax.all_to_all(
            dx.reshape(n_exp, capacity, width), "expert", split_axis=0, concat_axis=0, tiled=True
        ),
        lax.all_to_all(
            route.reshape(n_exp, capacity), "expert", split_axis=0, concat_axis=0, tiled=True
        ),
    )
    picked = back_rows.reshape(n_exp * capacity, width)[slots].reshape(tok, topk, width)
    token_grad = jnp.sum(picked.astype(jnp.float32), axis=1).astype(jnp.bfloat16)
    prob_grad = back_route.reshape(n_exp * capacity)[slots].reshape(tok, topk)
    grad_down = lax.psum_scatter(
        down_term[None].astype(jnp.bfloat16), "dp", scatter_dimension=1, tiled=True
    )
    return (token_grad, prob_grad, grad_down)


def solution(mesh):
    return jax.shard_map(
        shards,
        mesh=mesh,
        in_specs=(
            P(("dp", "expert"), "tensor"),
            P(("dp", "expert"), None),
            P(("dp", "expert"), None),
            P("dp", "expert", None, None),
            P("expert", "tensor", None),
            P("expert", "tensor", None),
            P("expert", None, "tensor"),
        ),
        out_specs=(
            P(("dp", "expert"), "tensor"),
            P(("dp", "expert"), None),
            P("expert", "dp", "tensor"),
        ),
        check_vma=False,
    )
```

profile of v0, /device:TPU:0, one launch (start us, length us, event | category | flops | bytes accessed | tf_op | source)
XLA Modules:
  0.0 138.1 jit_solution(12945080364776589570)
XLA Ops:
  8.0 0.8 broadcast_multiply_fusion
  8.9 0.9 copy.20
  10.0 0.8 copy.24
  11.2 1.2 reduce-window.6
  12.9 1.4 %scatter_custom_fusion = s32[320]{0:T(512)S(1)} fusion(s32[256]{0:T(256)S(1)} %bitcast.52, s32[256]{0:T(256)S(1)} %iota_add_fusion, s32[]{:T(128)} %constant.32.clone.1), kind=kCustom, calls=%fused_computation.62 | custom fusion | bytes 1284 | tf_op jit(solution)/shard_map/scatter | solution.py:35
  14.3 2.4 %gather_fusion = bf16[320]{0:T(512)(128)(2,1)S(1)} fusion(bf16[256]{0:T(256)(128)(2,1)S(1)} %reshape.114, s32[1024]{0:T(1024)S(1)} %get-tuple-element.14), kind=kCustom, calls=%fused_computation | custom fusion | bytes 2560 | tf_op jit(solution)/shard_map/gather | solution.py:40
  16.8 6.1 %gather_fusion.1 = bf16[320,2048]{1,0:T(8,128)(2,1)} fusion(bf16[128,2048]{1,0:T(8,128)(2,1)} %param.7, s32[1024]{0:T(1024)S(1)} %get-tuple-element.13), kind=kCustom, calls=%fused_computation.1 | custom fusion | bytes 2622720 | tf_op jit(solution)/shard_map/gather | solution.py:39
  22.9 2.5 %broadcast_select_fusion = bf16[4,80,2048]{2,1,0:T(8,128)(2,1)} fusion(bf16[4,80,2048]{2,1,0:T(8,128)(2,1)} %bitcast.46, pred[4,80]{1,0:T(4,128)(4,1)S(1)} %broadcast_in_dim.32), kind=kLoop, calls=%fused_computation.18 | loop fusion | flops 655360 | bytes 2621760 | tf_op jit(solution)/shard_map/jit(_where)/select_n | solution.py:39
  25.4 4.3 %all-to-all-start.1 = ((bf16[4,80,2048]{2,1,0:T(8,128)(2,1)}), bf16[4,80,2048]{2,1,0:T(8,128)(2,1)}, u32[]{:S(2)}, u32[]{:S(2)}) async-start(bf16[4,80,2048]{2,1,0:T(8,128)(2,1)} %broadcast_select_fusion), calls=%async_computation.1 | async-start | bytes 2621440 | tf_op jit(solution)/shard_map/all_to_all | solution.py:42
  30.4 17.3 %all-to-all-done.1 = bf16[4,80,2048]{2,1,0:T(8,128)(2,1)} async-done(((bf16[4,80,2048]{2,1,0:T(8,128)(2,1)}), bf16[4,80,2048]{2,1,0:T(8,128)(2,1)}, u32[]{:S(2)}, u32[]{:S(2)}) %all-to-all-start.1) | async-done | bytes 1310752 | tf_op jit(solution)/shard_map/all_to_all | solution.py:42
  47.7 3.2 %all-to-all-start = ((bf16[4,1,80]{2,1,0:T(2,128)(2,1)}), bf16[4,1,80]{2,1,0:T(2,128)(2,1)S(1)}, u32[]{:S(2)}, u32[]{:S(2)}) async-start(bf16[4,1,80]{2,1,0:T(2,128)(2,1)} %all_to_all.21), calls=%async_computation | async-start | bytes 4096 | tf_op jit(solution)/shard_map/all_to_all | solution.py:49
  50.9 4.3 %fusion.13 = bf16[320,768]{1,0:T(8,128)(2,1)} fusion(bf16[320,2048]{1,0:T(8,128)(2,1)} %bitcast.5, bf16[1,768,2048]{2,1,0:T(8,128)(2,1)} %param.13), kind=kOutput, calls=%fused_computation.19 | convolution fusion | flops 1006878720 | bytes 4947968 | tf_op jit(solution)/shard_map/dot_general | solution.py:65
  55.4 5.2 %fusion.6 = bf16[1,768,2048]{2,1,0:T(8,128)(2,1)} fusion(bf16[320,2048]{1,0:T(8,128)(2,1)} %bitcast.5, f32[320]{0:T(512)S(1)} %reshape.121, bf16[320,1536]{1,0:T(8,128)(2,1)} %bitcast.48), kind=kOutput, calls=%fused_computation.12 | convolution fusion | flops 1010417664 | bytes 5440768 | tf_op jit(solution)/shard_map/dot_general | solution.py:62
  60.7 25.1 %all-reduce.2.cloned.1.call-done = bf16[320,768]{1,0:T(8,128)(2,1)} async-done(((bf16[320,768]{1,0:T(8,128)(2,1)}), bf16[320,768]{1,0:T(8,128)(2,1)}) %all-reduce.2.cloned.1.call-update) | async-done | bytes 491536 | tf_op jit(solution)/shard_map/psum | solution.py:68
  85.8 1.8 %fusion.18 = bf16[320]{0:T(512)(128)(2,1)S(1)} fusion(bf16[320,768]{1,0:T(8,128)(2,1)} %all-reduce.2.cloned.1.call-done, bf16[320,1536]{1,0:T(8,128)(2,1)} %bitcast.49), kind=kLoop, calls=%fused_computation.26 | loop fusion | flops 2457280 | bytes 1475200 | tf_op jit(solution)/shard_map/reduce_sum | solution.py:16
  88.3 3.2 %all-to-all-start.3 = ((bf16[4,1,80]{2,1,0:T(2,128)(2,1)}), bf16[4,1,80]{2,1,0:T(2,128)(2,1)S(1)}, u32[]{:S(2)}, u32[]{:S(2)}) async-start(bf16[4,1,80]{2,1,0:T(2,128)(2,1)} %convert_element_type.81), calls=%async_computation.3 | async-start | bytes 4096 | tf_op jit(solution)/shard_map/all_to_all | solution.py:81
  91.5 2.7 %fusion = f32[320,2048]{1,0:T(8,128)S(1)} fusion(bf16[1,2048,768]{2,1,0:T(8,128)(2,1)S(1)} %copy-done, bf16[320,768]{1,0:T(8,128)(2,1)} %all-reduce.2.cloned.1.call-done, f32[320]{0:T(512)S(1)} %reshape.121, bf16[320,1536]{1,0:T(8,128)(2,1)} %bitcast.50), kind=kOutput, calls=%fused_computation.6 | convolution fusion | flops 1008844800 | bytes 6751488 | tf_op jit(solution)/shard_map/dot_general | solution.py:73
  94.3 2.6 %fusion.10 = bf16[320,2048]{1,0:T(8,128)(2,1)} fusion(f32[320,2048]{1,0:T(8,128)S(1)} %fusion, bf16[1,2048,768]{2,1,0:T(8,128)(2,1)S(1)} %copy-done.3, bf16[320,768]{1,0:T(8,128)(2,1)S(1)} %copy-done.2, f32[320]{0:T(512)S(1)} %reshape.121, bf16[320,1536]{1,0:T(8,128)(2,1)S(1)} %bitcast.51), kind=kOutput, calls=%fused_computation.14 | convolution fusion | flops 1011384320 | bytes 8553728 | tf_op jit(solution)/shard_map/dot_general | solution.py:70
  96.9 4.5 %all-to-all-start.2 = ((bf16[4,80,2048]{2,1,0:T(8,128)(2,1)}), bf16[4,80,2048]{2,1,0:T(8,128)(2,1)}, u32[]{:S(2)}, u32[]{:S(2)}) async-start(bf16[4,80,2048]{2,1,0:T(8,128)(2,1)} %bitcast.47), calls=%async_computation.2 | async-start | bytes 2621440 | tf_op jit(solution)/shard_map/all_to_all | solution.py:78
  101.5 1.9 %gather_fusion.3 = bf16[256]{0:T(256)(128)(2,1)S(1)} fusion(bf16[320]{0:T(512)(128)(2,1)S(1)} %reshape.119, s32[1024]{0:T(1024)S(1)} %pad_clamp_fusion), kind=kCustom, calls=%fused_computation.3 | custom fusion | bytes 2048 | tf_op jit(solution)/shard_map/gather | solution.py:87
  104.2 14.4 %all-to-all-done.2 = bf16[4,80,2048]{2,1,0:T(8,128)(2,1)} async-done(((bf16[4,80,2048]{2,1,0:T(8,128)(2,1)}), bf16[4,80,2048]{2,1,0:T(8,128)(2,1)}, u32[]{:S(2)}, u32[]{:S(2)}) %all-to-all-start.2) | async-done | bytes 1310752 | tf_op jit(solution)/shard_map/all_to_all | solution.py:78
  118.7 4.9 %gather_fusion.2 = bf16[256,2048]{1,0:T(8,128)(2,1)} fusion(bf16[320,2048]{1,0:T(8,128)(2,1)} %bitcast.11, s32[1024]{0:T(1024)S(1)} %pad_clamp_fusion), kind=kCustom, calls=%fused_computation.2 | custom fusion | bytes 2098176 | tf_op jit(solution)/shard_map/gather | solution.py:85
  123.5 2.5 %reshape.118 = bf16[128,2,2048]{2,1,0:T(2,128)(2,1)} reshape(bf16[256,2048]{1,0:T(8,128)(2,1)} %gather_fusion.2) | data formatting | bytes 2097152 | tf_op jit(solution)/shard_map/reshape | solution.py:85
  126.1 4.6 %reduce_sum.34 = bf16[128,2048]{1,0:T(8,128)(2,1)} reduce(bf16[128,2,2048]{2,1,0:T(2,128)(2,1)} %reshape.118, bf16[]{:T(256)} %constant.37.clone.1), dimensions={1}, to_apply=%region_5.6 | reduce | flops 262144 | bytes 1572866 | tf_op jit(solution)/shard_map/reduce_sum | solution.py:86
  (43 shorter events, 3.7 us)
Async XLA Ops:
  8.0 83.5 %copy-start = (bf16[1,2048,768]{2,1,0:T(8,128)(2,1)S(1)}, bf16[1,2048,768]{2,1,0:T(8,128)(2,1)}, u32[]{:S(2)}) copy-start(bf16[1,2048,768]{2,1,0:T(8,128)(2,1)} %param.12) | copy-start | bytes 9437188
  25.4 22.3 %all-to-all-start.1 = ((bf16[4,80,2048]{2,1,0:T(8,128)(2,1)}), bf16[4,80,2048]{2,1,0:T(8,128)(2,1)}, u32[]{:S(2)}, u32[]{:S(2)}) async-start(bf16[4,80,2048]{2,1,0:T(8,128)(2,1)} %broadcast_select_fusion), calls=%async_computation.1 | async-start | bytes 2621440 | tf_op jit(solution)/shard_map/all_to_all | solution.py:42
  47.7 7.6 %all-to-all-start = ((bf16[4,1,80]{2,1,0:T(2,128)(2,1)}), bf16[4,1,80]{2,1,0:T(2,128)(2,1)S(1)}, u32[]{:S(2)}, u32[]{:S(2)}) async-start(bf16[4,1,80]{2,1,0:T(2,128)(2,1)} %all_to_all.21), calls=%async_computation | async-start | bytes 4096 | tf_op jit(solution)/shard_map/all_to_all | solution.py:49
  50.9 34.9 %all-reduce.2.cloned.1.call-start = ((), (), s32[]{:S(2)}) async-start(), calls=%async_computation.5 | async-start | bytes 983040 | tf_op jit(solution)/shard_map/psum | solution.py:68
  55.3 75.4 %reduce-scatter.2.cloned.1.call-start = ((), (), s32[]{:S(2)}) async-start(), calls=%async_computation.6 | async-start | bytes 3932160 | tf_op jit(solution)/shard_map/reduce_scatter | solution.py:88
  88.3 8.7 %all-to-all-start.3 = ((bf16[4,1,80]{2,1,0:T(2,128)(2,1)}), bf16[4,1,80]{2,1,0:T(2,128)(2,1)S(1)}, u32[]{:S(2)}, u32[]{:S(2)}) async-start(bf16[4,1,80]{2,1,0:T(2,128)(2,1)} %convert_element_type.81), calls=%async_computation.3 | async-start | bytes 4096 | tf_op jit(solution)/shard_map/all_to_all | solution.py:81
  91.5 2.7 %copy-start.1 = (bf16[1,1,320,1536]{3,2,1,0:T(8,128)(2,1)S(1)}, bf16[1,1,320,1536]{3,2,1,0:T(8,128)(2,1)}, u32[]{:S(2)}) copy-start(bf16[1,1,320,1536]{3,2,1,0:T(8,128)(2,1)} %param.10) | copy-start | bytes 2949124
  91.5 2.7 %copy-start.2 = (bf16[320,768]{1,0:T(8,128)(2,1)S(1)}, bf16[320,768]{1,0:T(8,128)(2,1)}, u32[]{:S(2)}) copy-start(bf16[320,768]{1,0:T(8,128)(2,1)} %all-reduce.2.cloned.1.call-done) | copy-start | bytes 1474564
  91.5 2.7 %copy-start.3 = (bf16[1,2048,768]{2,1,0:T(8,128)(2,1)S(1)}, bf16[1,2048,768]{2,1,0:T(8,128)(2,1)}, u32[]{:S(2)}) copy-start(bf16[1,2048,768]{2,1,0:T(8,128)(2,1)} %param.11) | copy-start | bytes 9437188
  96.9 21.8 %all-to-all-start.2 = ((bf16[4,80,2048]{2,1,0:T(8,128)(2,1)}), bf16[4,80,2048]{2,1,0:T(8,128)(2,1)}, u32[]{:S(2)}, u32[]{:S(2)}) async-start(bf16[4,80,2048]{2,1,0:T(8,128)(2,1)} %bitcast.47), calls=%async_computation.2 | async-start | bytes 2621440 | tf_op jit(solution)/shard_map/all_to_all | solution.py:78
Sparse Core Ops, SparseCore 0:
  55.4 30.4 all-reduce.1
Sparse Core Ops, SparseCore 1:
  60.8 62.8 reduce-scatter.1
where the time goes:
time: 139 us; the launch traced here: 138 us
  waiting for transfers between devices  56.9 us (41%)
  local copies, waits for them, and re-layouts  24.2 us (17%)
  between operations  15.7 us (11%)
  starting transfers between devices  15.3 us (11%)
  matrix products  14.9 us (11%)
  other arithmetic  11.2 us (8%)
    psum x1, waiting for transfers between devices, shards(): lax.psum(dh_part.astype(jnp.bfloat16), 'tensor').astype(jnp.float32)  25.1 us
    all_to_all x1, waiting for transfers between devices, shards(): lax.all_to_all(send_rows.reshape(n_exp, capacity, width), 'expert', split...  17.3 us
    all_to_all x1, waiting for transfers between devices, shards(): lax.all_to_all(dx.reshape(n_exp, capacity, width), 'expert', split_axis=0...  14.4 us
    gather x1, local copies, waits for them, and re-layouts, shards(): grad_out[flat_src // topk]  6.07 us
    dot_general x1, matrix products, shards(): lax.dot_general(hpro, dyr, (((0,), (0,)), ((), ())), preferred_element_ty...  5.24 us
    gather x1, local copies, waits for them, and re-layouts, shards(): back_rows.reshape(n_exp * capacity, width)[slots].reshape(tok, topk, width)  4.86 us
    reduce_sum x1, other arithmetic, shards(): jnp.sum(picked.astype(jnp.float32), axis=1).astype(jnp.bfloat16)  4.57 us
    all_to_all x1, starting transfers between devices, shards(): lax.all_to_all(dx.reshape(n_exp, capacity, width), 'expert', split_axis=0...  4.47 us
  transfers between devices with their start and end apart: 6, of which 3 were waited for; matrix products, arithmetic and copies ran while one was open for 23% of the time, Pallas kernels for 0%

commit v1 on v0

--- a/solution.py
+++ b/solution.py
@@ -1,7 +1,379 @@
+import functools
+
 import jax
 import jax.numpy as jnp
 from jax import lax
+from jax.experimental import pallas as pl
+from jax.experimental.pallas import tpu as pltpu
 from jax.sharding import PartitionSpec as P
+
+MESH = pl.DeviceIdType.MESH
+BF16, F32 = jnp.bfloat16, jnp.float32
+LANES = 128
+
+
+def dot(a, b, ca=1, cb=0):
+    return lax.dot_general(a, b, (((ca,), (cb,)), ((), ())), preferred_element_type=F32)
+
+
+def fused(
+    n_z, cap, nb,
+    ids_ref, prob_ref, tok_hbm, pre_hbm, wg_hbm, wu_hbm, wd_hbm,
+    tg_ref, pg_ref, gd_ref,
+    tok, pre, wg, wu, wd,
+    onehot_t, meta_s, meta_r, rows_s, disp,
+    slope, act_v, hid_v, hp, hp_t,
+    dh, dh_s, dh_r, dg, du, dx, back, rt_s, rt_r,
+    up_s, up_r, lo_s, lo_r,
+    tok_sem, pre_sem, w_sem,
+    meta_ss, meta_rs, disp_ss, disp_rs, dh_ss, dh_rs, back_ss, back_rs, rt_ss, rt_rs,
+    up_ss, up_rs, lo_ss, lo_rs,
+):
+    z, me, x = lax.axis_index("dp"), lax.axis_index("expert"), lax.axis_index("tensor")
+    peer = [me, me + 1 - 2 * (me % 2), (me + 2) % 4, 3 - me]
+    far = (2, 3, 1)
+    tokens, width = tok.shape[0], tok.shape[1]
+    bw = width // nb
+    hidden = wd.shape[0]
+    piece = hidden // n_z
+
+    def rows(k):
+        return pl.ds(k * cap, cap)
+
+    def cols(j):
+        return pl.ds(j * bw, bw)
+
+    def to_peer(src, dst, ss, rs, k):
+        return pltpu.make_async_remote_copy(src, dst, ss, rs, device_id={"expert": peer[k]}, device_id_type=MESH)
+
+    def meta_copy(k):
+        return to_peer(meta_s.at[rows(k)], meta_r.at[rows(k)], meta_ss.at[k], meta_rs.at[k], k)
+
+    def disp_copy(k, j):
+        return to_peer(rows_s.at[j, rows(k)], disp.at[j, rows(k)], disp_ss.at[k, j], disp_rs.at[k, j], k)
+
+    def back_copy(k, j):
+        return to_peer(dx.at[j, rows(k)], back.at[j, rows(k)], back_ss.at[k, j], back_rs.at[k, j], k)
+
+    def rt_copy(k):
+        return to_peer(rt_s.at[rows(k)], rt_r.at[rows(k)], rt_ss.at[k], rt_rs.at[k], k)
+
+    def dh_copy(k):
+        return pltpu.make_async_remote_copy(
+            dh_s.at[rows(k)], dh_r.at[rows(k)], dh_ss.at[k], dh_rs.at[k],
+            device_id={"tensor": 1 - x}, device_id_type=MESH)
+
+    def up_copy(d, j):
+        return pltpu.make_async_remote_copy(
+            up_s.at[d, j], up_r.at[d, j], up_ss.at[d, j], up_rs.at[d, j],
+            device_id={"dp": z + 1}, device_id_type=MESH)
+
+    def lo_copy(d, j):
+        return pltpu.make_async_remote_copy(
+            lo_s.at[d, j], lo_r.at[d, j], lo_ss.at[d, j], lo_rs.at[d, j],
+            device_id={"dp": z - 1}, device_id_type=MESH)
+
+    tok_in = [pltpu.make_async_copy(tok_hbm.at[:, cols(j)], tok.at[:, cols(j)], tok_sem.at[j]) for j in range(nb)]
+    pre_in = [
+        pltpu.make_async_copy(pre_hbm.at[pl.ds(pl.multiple_of(peer[k] * cap, 16), cap)], pre.at[rows(k)], pre_sem.at[k])
+        for k in range(4)
+    ]
+    w_in = [
+        pltpu.make_async_copy(wd_hbm, wd, w_sem.at[0]),
+        pltpu.make_async_copy(wg_hbm, wg, w_sem.at[1]),
+        pltpu.make_async_copy(wu_hbm, wu, w_sem.at[2]),
+    ]
+    for c in tok_in + pre_in + w_in:
+        c.start()
+
+    barrier = pltpu.get_barrier_semaphore()
+    for k in (1, 2, 3):
+        pl.semaphore_signal(barrier, inc=1, device_id={"expert": peer[k]}, device_id_type=MESH)
+    pl.semaphore_signal(barrier, inc=1, device_id={"tensor": 1 - x}, device_id_type=MESH)
+
+    @pl.when(z > 0)
+    def _():
+        pl.semaphore_signal(barrier, inc=1, device_id={"dp": z - 1}, device_id_type=MESH)
+
+    @pl.when(z < n_z - 1)
+    def _():
+        pl.semaphore_signal(barrier, inc=1, device_id={"dp": z + 1}, device_id_type=MESH)
+
+    ids = ids_ref[...]
+    prb = prob_ref[...].astype(F32)
+    lane = lax.broadcasted_iota(jnp.int32, (tokens, LANES), 1)
+    row_i = lax.broadcasted_iota(jnp.int32, (tokens, tokens), 0)
+    col_i = lax.broadcasted_iota(jnp.int32, (tokens, tokens), 1)
+    lower = (col_i < row_i).astype(F32).astype(BF16)
+    first, second = ids[:, 0:1], ids[:, 1:2]
+    pick = []
+    for k in range(4):
+        m = ((first == peer[k]) | (second == peer[k])).astype(F32)
+        mb = jnp.broadcast_to(m, (tokens, LANES))
+        pos = dot(lower, mb.astype(BF16))
+        sel = jnp.where(pos == lane.astype(F32), mb, 0.0)
+        onehot_t[k] = sel.astype(BF16)
+        s = sel.T[:cap].astype(BF16)
+        pick.append(s)
+        pk = jnp.where(first == peer[k], prb[:, 0:1], jnp.where(second == peer[k], prb[:, 1:2], 0.0))
+        meta = dot(s, jnp.broadcast_to(pk, (tokens, LANES)).astype(BF16)).astype(BF16)
+        if k == 0:
+            meta_r[rows(0)] = meta
+        else:
+            meta_s[rows(k)] = meta
+
+    @pl.when((z > 0) & (z < n_z - 1))
+    def _():
+        pl.semaphore_wait(barrier, 6)
+
+    @pl.when((z == 0) | (z == n_z - 1))
+    def _():
+        pl.semaphore_wait(barrier, 5)
+
+    for k in far:
+        meta_copy(k).start()
+    for j in range(nb):
+        tok_in[j].wait()
+        block = tok[:, cols(j)]
+        for k in far:
+            rows_s[j, rows(k)] = dot(pick[k], block).astype(BF16)
+            disp_copy(k, j).start()
+        disp[j, rows(0)] = dot(pick[0], block).astype(BF16)
+
+    for k in range(4):
+        pre_in[k].wait()
+        if k:
+            meta_copy(k).wait_recv()
+        p = meta_r[rows(k)].astype(F32)[:, 0:1]
+        g = pre[rows(k), :hidden].astype(F32)
+        u = pre[rows(k), hidden:].astype(F32)
+        sg = jax.nn.sigmoid(g)
+        act = g * sg
+        hid = act * u
+        act_v[rows(k)] = act
+        hid_v[rows(k)] = hid
+        slope[rows(k)] = u * sg * (1.0 + g * (1.0 - sg))
+        hp[rows(k)] = p * hid
+    for h in range(0, hidden, LANES):
+        hp_t[pl.ds(h, LANES)] = hp[:, pl.ds(h, LANES)].T.astype(BF16)
+
+    def product(d, j):
+        return dot(hp_t[pl.ds(pl.multiple_of(d * piece, 16), piece)], disp[j])
+
+    def send_up(d, j, inner):
+        v = product(d, j)
+        if inner:
+            up_copy(d, j).wait_recv()
+            v = v + up_r[d, j].astype(F32)
+        up_s[d, j] = v.astype(BF16)
+        up_copy(d, j).start()
+
+    def send_lo(d, j, inner):
+        v = product(d, j)
+        if inner:
+            lo_copy(d, j).wait_recv()
+            v = v + lo_r[d, j].astype(F32)
+        lo_s[d, j] = v.astype(BF16)
+        lo_copy(d, j).start()
+
+    w_in[0].wait()
+    for j in range(nb):
+        for k in far:
+            disp_copy(k, j).wait_recv()
+
+        @pl.when(z == 0)
+        def _():
+            send_up(n_z - 1, j, False)
+
+        @pl.when(z == n_z - 1)
+        def _():
+            send_lo(0, j, False)
+
+        part = dot(disp[j], wd[:, cols(j)], 1, 1)
+        if j == 0:
+            dh[...] = part
+        elif j < nb - 1:
+            dh[...] += part
+        else:
+            part = (dh[...] + part).astype(BF16)
+            dh_s[...] = part
+    for k in (2, 3, 1, 0):
+        dh_copy(k).start()
+
+    @pl.when(z == 0)
+    def _():
+        for d in range(n_z - 2, 0, -1):
+            for j in range(nb):
+                send_up(d, j, False)
+
+    @pl.when(z == n_z - 1)
+    def _():
+        for d in range(1, n_z - 1):
+            for j in range(nb):
+                send_lo(d, j, False)
+
+    def inner_step(t, blocks):
+        for j in blocks:
+            @pl.when((z > 0) & (z < n_z - 1 - t))
+            def _():
+                send_up(n_z - 1 - t, j, True)
+
+            @pl.when((z < n_z - 1) & (z > t))
+            def _():
+                send_lo(t, j, True)
+
+    def input_grad(pair):
+        lo = min(pair) * cap
+        for k in pair:
+            dh_copy(k).wait_recv()
+            d = dh_s[rows(k)].astype(F32) + dh_r[rows(k)].astype(F32)
+            route = jnp.sum(d * hid_v[rows(k)], axis=1, keepdims=True)
+            route = jnp.broadcast_to(route, (cap, LANES)).astype(BF16)
+            a = meta_r[rows(k)].astype(F32)[:, 0:1] * d
+            dg[rows(k)] = (a * slope[rows(k)]).astype(BF16)
+            du[rows(k)] = (a * act_v[rows(k)]).astype(BF16)
+            if k:
+                rt_s[rows(k)] = route
+                rt_copy(k).start()
+            else:
+                rt_r[rows(0)] = route
+        both = pl.ds(lo, 2 * cap)
+        for j in range(nb):
+            v = dot(dg[both], wg[cols(j)], 1, 1) + dot(du[both], wu[cols(j)], 1, 1)
+            v = v.astype(BF16)
+            dx[j, both] = v
+            for k in pair:
+                if k:
+                    back_copy(k, j).start()
+
+    inner_step(0, range(0, nb // 2))
+    w_in[1].wait()
+    w_in[2].wait()
+    input_grad((2, 3))
+    inner_step(0, range(nb // 2, nb))
+    input_grad((1, 0))
+    for t in range(1, n_z - 1):
+        inner_step(t, range(nb))
+
+    for j in range(nb):
+        v = dot(onehot_t[0, :, :cap], dx[j, rows(0)])
+        for k in (1, 2, 3):
+            back_copy(k, j).wait_recv()
+            v = v + dot(onehot_t[k, :, :cap], back[j, rows(k)])
+        tg_ref[:, cols(j)] = v.astype(BF16)
+    v0 = jnp.zeros((tokens, LANES), F32)
+    v1 = jnp.zeros((tokens, LANES), F32)
+    for k in range(4):
+        if k:
+            rt_copy(k).wait_recv()
+        r = dot(onehot_t[k, :, :cap], rt_r[rows(k)])
+        v0 = v0 + jnp.where(first == peer[k], r, 0.0)
+        v1 = v1 + jnp.where(second == peer[k], r, 0.0)
+    pg_ref[...] = jnp.where(lane == 0, v0, v1)[:, :2].astype(BF16)
+
+    own = z
+    for j in range(nb):
+        hold = dh.at[pl.ds(0, piece), pl.ds(0, bw)]
+        hold[...] = product(own, j)
+
+        @pl.when(z > 0)
+        def _():
+            up_copy(own, j).wait_recv()
+            hold[...] += up_r[own, j].astype(F32)
+
+        @pl.when(z < n_z - 1)
+        def _():
+            lo_copy(own, j).wait_recv()
+            hold[...] += lo_r[own, j].astype(F32)
+
+        gd_ref[:, cols(j)] = hold[...].astype(BF16)
+
+    for k in (1, 2, 3):
+        meta_copy(k).wait_send()
+        rt_copy(k).wait_send()
+        for j in range(nb):
+            disp_copy(k, j).wait_send()
+            back_copy(k, j).wait_send()
+    for k in range(4):
+        dh_copy(k).wait_send()
+    for d in range(n_z):
+        for j in range(nb):
+            @pl.when(z < d)
+            def _():
+                up_copy(d, j).wait_send()
+
+            @pl.when(z > d)
+            def _():
+                lo_copy(d, j).wait_send()
+
+
+def fused_shards(n_z, grad_out, route_ids, route_probs, saved_pre, w_gate, w_up, w_down):
+    tok, width = grad_out.shape
+    slot_rows = saved_pre.shape[2]
+    cap = slot_rows // 4
+    hidden = saved_pre.shape[3] // 2
+    nb = 4
+    bw = width // nb
+    piece = hidden // n_z
+    vmem = pl.BlockSpec(memory_space=pltpu.VMEM)
+    hbm = pl.BlockSpec(memory_space=pl.ANY)
+    dma = pltpu.SemaphoreType.DMA
+    blocks = (nb, slot_rows, bw)
+    hops = (n_z, nb, piece, bw)
+    return pl.pallas_call(
+        functools.partial(fused, n_z, cap, nb),
+        out_shape=(
+            jax.ShapeDtypeStruct((tok, width), BF16),
+            jax.ShapeDtypeStruct(route_probs.shape, BF16),
+            jax.ShapeDtypeStruct((piece, width), BF16),
+        ),
+        in_specs=[vmem, vmem, hbm, hbm, hbm, hbm, hbm],
+        out_specs=(vmem, vmem, vmem),
+        scratch_shapes=[
+            pltpu.VMEM((tok, width), BF16),
+            pltpu.VMEM((slot_rows, 2 * hidden), BF16),
+            pltpu.VMEM((width, hidden), BF16),
+            pltpu.VMEM((width, hidden), BF16),
+            pltpu.VMEM((hidden, width), BF16),
+            pltpu.VMEM((4, tok, LANES), BF16),
+            pltpu.VMEM((slot_rows, LANES), BF16),
+            pltpu.VMEM((slot_rows, LANES), BF16),
+            pltpu.VMEM(blocks, BF16),
+            pltpu.VMEM(blocks, BF16),
+            pltpu.VMEM((slot_rows, hidden), F32),
+            pltpu.VMEM((slot_rows, hidden), F32),
+            pltpu.VMEM((slot_rows, hidden), F32),
+            pltpu.VMEM((slot_rows, hidden), F32),
+            pltpu.VMEM((hidden, slot_rows), BF16),
+            pltpu.VMEM((slot_rows, hidden), F32),
+            pltpu.VMEM((slot_rows, hidden), BF16),
+            pltpu.VMEM((slot_rows, hidden), BF16),
+            pltpu.VMEM((slot_rows, hidden), BF16),
+            pltpu.VMEM((slot_rows, hidden), BF16),
+            pltpu.VMEM(blocks, BF16),
+            pltpu.VMEM(blocks, BF16),
+            pltpu.VMEM((slot_rows, LANES), BF16),
+            pltpu.VMEM((slot_rows, LANES), BF16),
+            pltpu.VMEM(hops, BF16),
+            pltpu.VMEM(hops, BF16),
+            pltpu.VMEM(hops, BF16),
+            pltpu.VMEM(hops, BF16),
+            dma((nb,)), dma((4,)), dma((3,)),
+            dma((4,)), dma((4,)), dma((4, nb)), dma((4, nb)), dma((4,)), dma((4,)),
+            dma((4, nb)), dma((4, nb)), dma((4,)), dma((4,)),
+            dma((n_z, nb)), dma((n_z, nb)), dma((n_z, nb)), dma((n_z, nb)),
+        ],
+        compiler_params=pltpu.CompilerParams(
+            collective_id=0, has_side_effects=True, vmem_limit_bytes=56 * 1024 * 1024
+        ),
+    )(route_ids, route_probs, grad_out, saved_pre[0, 0], w_gate[0], w_up[0], w_down[0])
+
+
+def takes_fused(shape, width, hidden, capacity):
+    return (
+        shape["expert"] == 4 and shape["tensor"] == 2 and shape["dp"] > 1 and capacity % 16 == 0 and capacity <= LANES
+        and width % (4 * LANES) == 0 and hidden % LANES == 0 and (hidden // shape["dp"]) % 16 == 0
+    )
 
 
 def slot_index(id_block, n_experts, capacity):
@@ -92,8 +464,20 @@
 
 
 def solution(mesh):
+    shape = dict(mesh.shape)
+
+    def local(*args):
+        saved_pre, w_down = args[3], args[6]
+        capacity = saved_pre.shape[2] // shape["expert"]
+        tok = args[0].shape[0]
+        if tok == LANES and takes_fused(shape, w_down.shape[2], w_down.shape[1], capacity):
+            return tuple(
+                v[None] if i == 2 else v for i, v in enumerate(fused_shards(shape["dp"], *args))
+            )
+        return shards(*args)
+
     return jax.shard_map(
-        shards,
+        local,
         mesh=mesh,
         in_specs=(
             P(("dp", "expert"), "tensor"),

time: 139 us -> 98.3 us (0.71)
  the two profiles are of different devices: /device:TPU:0 before, /device:TPU:16 now
where the time goes in v1:
time: 98.3 us; the launch traced here: 98 us
  Pallas kernels  89.2 us (91%)
  local copies, waits for them, and re-layouts  8.11 us (8%)
    pallas_call x1, Pallas kernels, fused_shards(): pl.pallas_call(functools.partial(fused, n_z, cap, nb), out_shape=(jax.Sha...  89.2 us
    unnamed x5, local copies, waits for them, and re-layouts  8.11 us

profile of v1, /device:TPU:16, one launch (start us, length us, event | category | flops | bytes accessed | tf_op | source)
XLA Modules:
  0.0 98.0 jit_solution(6351305726871077251)
XLA Ops:
  0.6 1.4 %copy.11.prob_ref = bf16[128,2]{1,0:T(8,128)(2,1)} copy(bf16[128,2]{0,1:T(2,128)(2,1)} %param.9) | data formatting | bytes 1024 | tf_op args[2]
  2.0 1.4 %copy.10.ids_ref = s32[128,2]{1,0:T(8,128)} copy(s32[128,2]{0,1:T(2,128)} %param.8) | data formatting | bytes 2048 | tf_op args[1]
  3.4 89.2 %shard_map.94 = (bf16[128,2048]{1,0:T(8,128)(2,1)}, bf16[128,2]{1,0:T(8,128)(2,1)}, bf16[192,2048]{1,0:T(8,128)(2,1)}) custom-call(s32[128,2]{1,0:T(8,128)} %copy.10.ids_ref, bf16[128,2]{1,0:T(8,128)(2,1)} %copy.11.prob_ref, bf16[128,2048]{1,0:T(8,128)(2,1)} %tok_hbm.1, bf16[320,1536]{1,0:T(8,128)(2,1)} %bitcast.8, bf16[2048,768]{1,0:T(8,128)(2,1)} %bitcast.5, ...), custom_call_target="tpu_custom_call" | custom-call | tf_op jit(solution)/shard_map/pallas_call | solution.py:323
  92.7 1.4 %copy.12 = bf16[128,2]{0,1:T(2,128)(2,1)} copy(bf16[128,2]{1,0:T(8,128)(2,1)} %get-tuple-element.10) | data formatting | bytes 1024
  94.0 1.9 %copy.15 = bf16[128,2048]{1,0:T(8,128)(2,1)} copy(bf16[128,2048]{1,0:T(8,128)(2,1)} %get-tuple-element.15) | data formatting | bytes 1048576
  95.9 2.1 %copy.16 = bf16[1,192,2048]{2,1,0:T(8,128)(2,1)} copy(bf16[1,192,2048]{2,1,0:T(8,128)(2,1)} %bitcast.9) | data formatting | bytes 1572864

commit v2 on v1

--- a/solution.py
+++ b/solution.py
@@ -18,16 +18,16 @@
 
 def fused(
     n_z, cap, nb,
-    ids_ref, prob_ref, tok_hbm, pre_hbm, wg_hbm, wu_hbm, wd_hbm,
+    names_ref, tok_hbm, pre_hbm, wg_hbm, wu_hbm, wd_hbm,
     tg_ref, pg_ref, gd_ref,
     tok, pre, wg, wu, wd,
     onehot_t, meta_s, meta_r, rows_s, disp,
     slope, act_v, hid_v, hp, hp_t,
     dh, dh_s, dh_r, dg, du, dx, back, rt_s, rt_r,
-    up_s, up_r, lo_s, lo_r,
+    up_s, up_r, lo_s, lo_r, far_disp, far_hp,
     tok_sem, pre_sem, w_sem,
     meta_ss, meta_rs, disp_ss, disp_rs, dh_ss, dh_rs, back_ss, back_rs, rt_ss, rt_rs,
-    up_ss, up_rs, lo_ss, lo_rs,
+    up_ss, up_rs, lo_ss, lo_rs, end_ss, end_rs,
 ):
     z, me, x = lax.axis_index("dp"), lax.axis_index("expert"), lax.axis_index("tensor")
     peer = [me, me + 1 - 2 * (me % 2), (me + 2) % 4, 3 - me]
@@ -72,6 +72,26 @@
         return pltpu.make_async_remote_copy(
             lo_s.at[d, j], lo_r.at[d, j], lo_ss.at[d, j], lo_rs.at[d, j],
             device_id={"dp": z - 1}, device_id_type=MESH)
+
+    def end_copy(j, step):
+        return pltpu.make_async_remote_copy(
+            disp.at[j], far_disp.at[j], end_ss.at[j], end_rs.at[j],
+            device_id={"dp": z + step}, device_id_type=MESH)
+
+    def end_hp_copy(step):
+        part = pl.ds(piece if step > 0 else 0, hidden - piece)
+        return pltpu.make_async_remote_copy(
+            hp_t.at[part], far_hp.at[part], end_ss.at[nb], end_rs.at[nb],
+            device_id={"dp": z + step}, device_id_type=MESH)
+
+    def at_ends(act):
+        @pl.when(z == 0)
+        def _():
+            act(1)
+
+        @pl.when(z == n_z - 1)
+        def _():
+            act(-1)
 
     tok_in = [pltpu.make_async_copy(tok_hbm.at[:, cols(j)], tok.at[:, cols(j)], tok_sem.at[j]) for j in range(nb)]
     pre_in = [
@@ -99,8 +119,8 @@
     def _():
         pl.semaphore_signal(barrier, inc=1, device_id={"dp": z + 1}, device_id_type=MESH)
 
-    ids = ids_ref[...]
-    prb = prob_ref[...].astype(F32)
+    names = names_ref[...]
+    ids, prb = names[:, 0:2].astype(jnp.int32), names[:, 2:4]
     lane = lax.broadcasted_iota(jnp.int32, (tokens, LANES), 1)
     row_i = lax.broadcasted_iota(jnp.int32, (tokens, tokens), 0)
     col_i = lax.broadcasted_iota(jnp.int32, (tokens, tokens), 1)
@@ -160,11 +180,16 @@
     def product(d, j):
         return dot(hp_t[pl.ds(pl.multiple_of(d * piece, 16), piece)], disp[j])
 
+    def far_product(d, j):
+        return dot(far_hp[pl.ds(pl.multiple_of(d * piece, 16), piece)], far_disp[j])
+
     def send_up(d, j, inner):
         v = product(d, j)
         if inner:
             up_copy(d, j).wait_recv()
             v = v + up_r[d, j].astype(F32)
+        else:
+            v = v + far_product(d, j)
         up_s[d, j] = v.astype(BF16)
         up_copy(d, j).start()
 
@@ -173,22 +198,19 @@
         if inner:
             lo_copy(d, j).wait_recv()
             v = v + lo_r[d, j].astype(F32)
+        else:
+            v = v + far_product(d, j)
         lo_s[d, j] = v.astype(BF16)
         lo_copy(d, j).start()
 
+    at_ends(lambda step: end_hp_copy(step).start())
     w_in[0].wait()
     for j in range(nb):
         for k in far:
             disp_copy(k, j).wait_recv()
 
-        @pl.when(z == 0)
-        def _():
-            send_up(n_z - 1, j, False)
-
-        @pl.when(z == n_z - 1)
-        def _():
-            send_lo(0, j, False)
-
+        if j < 2:
+            at_ends(lambda step: end_copy(j, step).start())
         part = dot(disp[j], wd[:, cols(j)], 1, 1)
         if j == 0:
             dh[...] = part
@@ -200,25 +222,37 @@
     for k in (2, 3, 1, 0):
         dh_copy(k).start()
 
-    @pl.when(z == 0)
-    def _():
-        for d in range(n_z - 2, 0, -1):
-            for j in range(nb):
+    def end_next(j):
+        def go(step):
+            end_copy(j - 2, step).wait_send()
+            end_copy(j, step).start()
+
+        at_ends(go)
+
+    def far_step(j):
+        @pl.when(z == 1)
+        def _():
+            if j == 0:
+                end_hp_copy(1).wait_recv()
+            end_copy(j, 1).wait_recv()
+            for d in range(n_z - 1, 1, -1):
                 send_up(d, j, False)
 
-    @pl.when(z == n_z - 1)
-    def _():
-        for d in range(1, n_z - 1):
-            for j in range(nb):
+        @pl.when(z == n_z - 2)
+        def _():
+            if j == 0:
+                end_hp_copy(-1).wait_recv()
+            end_copy(j, -1).wait_recv()
+            for d in range(n_z - 2):
                 send_lo(d, j, False)
 
-    def inner_step(t, blocks):
-        for j in blocks:
-            @pl.when((z > 0) & (z < n_z - 1 - t))
+    def inner_step(j):
+        for t in range(n_z - 3):
+            @pl.when((z > 1) & (z < n_z - 1 - t))
             def _():
                 send_up(n_z - 1 - t, j, True)
 
-            @pl.when((z < n_z - 1) & (z > t))
+            @pl.when((z < n_z - 2) & (z > t))
             def _():
                 send_lo(t, j, True)
 
@@ -246,14 +280,19 @@
                 if k:
                     back_copy(k, j).start()
 
-    inner_step(0, range(0, nb // 2))
+    far_step(0)
+    end_next(2)
     w_in[1].wait()
     w_in[2].wait()
     input_grad((2, 3))
-    inner_step(0, range(nb // 2, nb))
+    end_next(3)
+    inner_step(0)
+    far_step(1)
     input_grad((1, 0))
-    for t in range(1, n_z - 1):
-        inner_step(t, range(nb))
+    for j in range(2, nb):
+        inner_step(j - 1)
+        far_step(j)
+    inner_step(nb - 1)
 
     for j in range(nb):
         v = dot(onehot_t[0, :, :cap], dx[j, rows(0)])
@@ -276,12 +315,16 @@
         hold = dh.at[pl.ds(0, piece), pl.ds(0, bw)]
         hold[...] = product(own, j)
 
-        @pl.when(z > 0)
+        @pl.when((z == 1) | (z == n_z - 2))
+        def _():
+            hold[...] += far_product(own, j)
+
+        @pl.when(z > 1)
         def _():
             up_copy(own, j).wait_recv()
             hold[...] += up_r[own, j].astype(F32)
 
-        @pl.when(z < n_z - 1)
+        @pl.when(z < n_z - 2)
         def _():
             lo_copy(own, j).wait_recv()
             hold[...] += lo_r[own, j].astype(F32)
@@ -298,13 +341,20 @@
         dh_copy(k).wait_send()
     for d in range(n_z):
         for j in range(nb):
-            @pl.when(z < d)
+            @pl.when((z > 0) & (z < d))
             def _():
                 up_copy(d, j).wait_send()
 
-            @pl.when(z > d)
+            @pl.when((z < n_z - 1) & (z > d))
             def _():
                 lo_copy(d, j).wait_send()
+
+    def ends_sent(step):
+        end_hp_copy(step).wait_send()
+        for j in range(nb - 2, nb):
+            end_copy(j, step).wait_send()
+
+    at_ends(ends_sent)
 
 
 def fused_shards(n_z, grad_out, route_ids, route_probs, saved_pre, w_gate, w_up, w_down):
@@ -315,6 +365,7 @@
     nb = 4
     bw = width // nb
     piece = hidden // n_z
+    names = jnp.concatenate([route_ids.astype(F32), route_probs.astype(F32)], axis=1)
     vmem = pl.BlockSpec(memory_space=pltpu.VMEM)
     hbm = pl.BlockSpec(memory_space=pl.ANY)
     dma = pltpu.SemaphoreType.DMA
@@ -327,7 +378,7 @@
             jax.ShapeDtypeStruct(route_probs.shape, BF16),
             jax.ShapeDtypeStruct((piece, width), BF16),
         ),
-        in_specs=[vmem, vmem, hbm, hbm, hbm, hbm, hbm],
+        in_specs=[vmem, hbm, hbm, hbm, hbm, hbm],
         out_specs=(vmem, vmem, vmem),
         scratch_shapes=[
             pltpu.VMEM((tok, width), BF16),
@@ -358,20 +409,22 @@
             pltpu.VMEM(hops, BF16),
             pltpu.VMEM(hops, BF16),
             pltpu.VMEM(hops, BF16),
+            pltpu.VMEM(blocks, BF16),
+            pltpu.VMEM((hidden, slot_rows), BF16),
             dma((nb,)), dma((4,)), dma((3,)),
             dma((4,)), dma((4,)), dma((4, nb)), dma((4, nb)), dma((4,)), dma((4,)),
             dma((4, nb)), dma((4, nb)), dma((4,)), dma((4,)),
-            dma((n_z, nb)), dma((n_z, nb)), dma((n_z, nb)), dma((n_z, nb)),
+            dma((n_z, nb)), dma((n_z, nb)), dma((n_z, nb)), dma((n_z, nb)), dma((nb + 1,)), dma((nb + 1,)),
         ],
         compiler_params=pltpu.CompilerParams(
             collective_id=0, has_side_effects=True, vmem_limit_bytes=56 * 1024 * 1024
         ),
-    )(route_ids, route_probs, grad_out, saved_pre[0, 0], w_gate[0], w_up[0], w_down[0])
+    )(names, grad_out, saved_pre[0, 0], w_gate[0], w_up[0], w_down[0])
 
 
 def takes_fused(shape, width, hidden, capacity):
     return (
-        shape["expert"] == 4 and shape["tensor"] == 2 and shape["dp"] > 1 and capacity % 16 == 0 and capacity <= LANES
+        shape["expert"] == 4 and shape["tensor"] == 2 and shape["dp"] > 3 and capacity % 16 == 0 and capacity <= LANES
         and width % (4 * LANES) == 0 and hidden % LANES == 0 and (hidden // shape["dp"]) % 16 == 0
     )
 

time: 98.3 us -> 77 us (0.78)
  the two profiles are of different devices: /device:TPU:16 before, /device:TPU:0 now
where the time goes in v2:
time: 77 us; the launch traced here: 76.7 us
  Pallas kernels  68.6 us (89%)
  local copies, waits for them, and re-layouts  6.06 us (8%)
  other arithmetic  1.35 us (2%)
    pallas_call x1, Pallas kernels, fused_shards(): pl.pallas_call(functools.partial(fused, n_z, cap, nb), out_shape=(jax.Sha...  68.6 us
    unnamed x3, local copies, waits for them, and re-layouts  5.32 us

profile of v2, /device:TPU:0, one launch (start us, length us, event | category | flops | bytes accessed | tf_op | source)
XLA Modules:
  0.0 76.7 jit_solution(3546141868171774360)
XLA Ops:
  0.6 0.7 convert_element_type.6
  1.3 0.7 convert_element_type.7
  2.0 0.7 copy.13.names_ref
  2.7 68.6 %shard_map.94 = (bf16[128,2048]{1,0:T(8,128)(2,1)}, bf16[128,2]{1,0:T(8,128)(2,1)}, bf16[192,2048]{1,0:T(8,128)(2,1)}) custom-call(f32[128,4]{1,0:T(8,128)} %copy.13.names_ref, bf16[128,2048]{1,0:T(8,128)(2,1)} %tok_hbm.1, bf16[320,1536]{1,0:T(8,128)(2,1)} %bitcast.8, bf16[2048,768]{1,0:T(8,128)(2,1)} %bitcast.5, bf16[2048,768]{1,0:T(8,128)(2,1)} %bitcast.6, ...), custom_call_target="tpu_custom_call" | custom-call | tf_op jit(solution)/shard_map/pallas_call | solution.py:374
  71.3 1.4 %copy.14 = bf16[128,2]{0,1:T(2,128)(2,1)} copy(bf16[128,2]{1,0:T(8,128)(2,1)} %get-tuple-element.13) | data formatting | bytes 1024
  72.7 1.9 %copy.17 = bf16[128,2048]{1,0:T(8,128)(2,1)} copy(bf16[128,2048]{1,0:T(8,128)(2,1)} %get-tuple-element.18) | data formatting | bytes 1048576
  74.6 2.1 %copy.18 = bf16[1,192,2048]{2,1,0:T(8,128)(2,1)} copy(bf16[1,192,2048]{2,1,0:T(8,128)(2,1)} %bitcast.9) | data formatting | bytes 1572864
  (1 shorter events, 0.0 us)

commit v3 on v2

--- a/solution.py
+++ b/solution.py
@@ -10,6 +10,7 @@
 MESH = pl.DeviceIdType.MESH
 BF16, F32 = jnp.bfloat16, jnp.float32
 LANES = 128
+BLOCKS = 8
 
 
 def dot(a, b, ca=1, cb=0):
@@ -18,7 +19,7 @@
 
 def fused(
     n_z, cap, nb,
-    names_ref, tok_hbm, pre_hbm, wg_hbm, wu_hbm, wd_hbm,
+    ids_ref, prob_ref, tok_hbm, pre_hbm, wg_hbm, wu_hbm, wd_hbm,
     tg_ref, pg_ref, gd_ref,
     tok, pre, wg, wu, wd,
     onehot_t, meta_s, meta_r, rows_s, disp,
@@ -36,6 +37,7 @@
     bw = width // nb
     hidden = wd.shape[0]
     piece = hidden // n_z
+    q = nb // 4
 
     def rows(k):
         return pl.ds(k * cap, cap)
@@ -119,24 +121,27 @@
     def _():
         pl.semaphore_signal(barrier, inc=1, device_id={"dp": z + 1}, device_id_type=MESH)
 
-    names = names_ref[...]
-    ids, prb = names[:, 0:2].astype(jnp.int32), names[:, 2:4]
     lane = lax.broadcasted_iota(jnp.int32, (tokens, LANES), 1)
     row_i = lax.broadcasted_iota(jnp.int32, (tokens, tokens), 0)
     col_i = lax.broadcasted_iota(jnp.int32, (tokens, tokens), 1)
     lower = (col_i < row_i).astype(F32).astype(BF16)
-    first, second = ids[:, 0:1], ids[:, 1:2]
+
+    def column(ref, i):
+        return jnp.broadcast_to(ref[i:i + 1, :].astype(F32), (tokens, tokens)).T
+
+    first, second = column(ids_ref, 0).astype(jnp.int32), column(ids_ref, 1).astype(jnp.int32)
+    prob0, prob1 = column(prob_ref, 0), column(prob_ref, 1)
     pick = []
     for k in range(4):
         m = ((first == peer[k]) | (second == peer[k])).astype(F32)
-        mb = jnp.broadcast_to(m, (tokens, LANES))
+        mb = m
         pos = dot(lower, mb.astype(BF16))
         sel = jnp.where(pos == lane.astype(F32), mb, 0.0)
         onehot_t[k] = sel.astype(BF16)
         s = sel.T[:cap].astype(BF16)
         pick.append(s)
-        pk = jnp.where(first == peer[k], prb[:, 0:1], jnp.where(second == peer[k], prb[:, 1:2], 0.0))
-        meta = dot(s, jnp.broadcast_to(pk, (tokens, LANES)).astype(BF16)).astype(BF16)
+        pk = jnp.where(first == peer[k], prob0, jnp.where(second == peer[k], prob1, 0.0))
+        meta = dot(s, pk.astype(BF16)).astype(BF16)
         if k == 0:
             meta_r[rows(0)] = meta
         else:
@@ -209,7 +214,7 @@
         for k in far:
             disp_copy(k, j).wait_recv()
 
-        if j < 2:
+        if j < 2 * q:
             at_ends(lambda step: end_copy(j, step).start())
         part = dot(disp[j], wd[:, cols(j)], 1, 1)
         if j == 0:
@@ -224,7 +229,7 @@
 
     def end_next(j):
         def go(step):
-            end_copy(j - 2, step).wait_send()
+            end_copy(j - 2 * q, step).wait_send()
             end_copy(j, step).start()
 
         at_ends(go)
@@ -280,19 +285,22 @@
                 if k:
                     back_copy(k, j).start()
 
-    far_step(0)
-    end_next(2)
+    for j in range(q):
+        far_step(j)
+        end_next(2 * q + j)
     w_in[1].wait()
     w_in[2].wait()
     input_grad((2, 3))
-    end_next(3)
-    inner_step(0)
-    far_step(1)
+    for j in range(q):
+        end_next(3 * q + j)
+        inner_step(j)
+        far_step(q + j)
     input_grad((1, 0))
-    for j in range(2, nb):
-        inner_step(j - 1)
+    for j in range(2 * q, nb):
+        inner_step(j - q)
         far_step(j)
-    inner_step(nb - 1)
+    for j in range(nb - q, nb):
+        inner_step(j)
 
     for j in range(nb):
         v = dot(onehot_t[0, :, :cap], dx[j, rows(0)])
@@ -308,7 +316,7 @@
         r = dot(onehot_t[k, :, :cap], rt_r[rows(k)])
         v0 = v0 + jnp.where(first == peer[k], r, 0.0)
         v1 = v1 + jnp.where(second == peer[k], r, 0.0)
-    pg_ref[...] = jnp.where(lane == 0, v0, v1)[:, :2].astype(BF16)
+    pg_ref[...] = jnp.where(row_i == 0, v0.T, v1.T)[:2].astype(BF16)
 
     own = z
     for j in range(nb):
@@ -351,7 +359,7 @@
 
     def ends_sent(step):
         end_hp_copy(step).wait_send()
-        for j in range(nb - 2, nb):
+        for j in range(nb - 2 * q, nb):
             end_copy(j, step).wait_send()
 
     at_ends(ends_sent)
@@ -362,10 +370,9 @@
     slot_rows = saved_pre.shape[2]
     cap = slot_rows // 4
     hidden = saved_pre.shape[3] // 2
-    nb = 4
+    nb = BLOCKS
     bw = width // nb
     piece = hidden // n_z
-    names = jnp.concatenate([route_ids.astype(F32), route_probs.astype(F32)], axis=1)
     vmem = pl.BlockSpec(memory_space=pltpu.VMEM)
     hbm = pl.BlockSpec(memory_space=pl.ANY)
     dma = pltpu.SemaphoreType.DMA
@@ -375,10 +382,10 @@
         functools.partial(fused, n_z, cap, nb),
         out_shape=(
             jax.ShapeDtypeStruct((tok, width), BF16),
-            jax.ShapeDtypeStruct(route_probs.shape, BF16),
+            jax.ShapeDtypeStruct(route_probs.shape[::-1], BF16),
             jax.ShapeDtypeStruct((piece, width), BF16),
         ),
-        in_specs=[vmem, hbm, hbm, hbm, hbm, hbm],
+        in_specs=[vmem, vmem, hbm, hbm, hbm, hbm, hbm],
         out_specs=(vmem, vmem, vmem),
         scratch_shapes=[
             pltpu.VMEM((tok, width), BF16),
@@ -419,13 +426,13 @@
         compiler_params=pltpu.CompilerParams(
             collective_id=0, has_side_effects=True, vmem_limit_bytes=56 * 1024 * 1024
         ),
-    )(names, grad_out, saved_pre[0, 0], w_gate[0], w_up[0], w_down[0])
+    )(route_ids.T, route_probs.T, grad_out, saved_pre[0, 0], w_gate[0], w_up[0], w_down[0])
 
 
 def takes_fused(shape, width, hidden, capacity):
     return (
         shape["expert"] == 4 and shape["tensor"] == 2 and shape["dp"] > 3 and capacity % 16 == 0 and capacity <= LANES
-        and width % (4 * LANES) == 0 and hidden % LANES == 0 and (hidden // shape["dp"]) % 16 == 0
+        and width % (BLOCKS * LANES) == 0 and hidden % LANES == 0 and (hidden // shape["dp"]) % 16 == 0
     )
 
 
@@ -525,7 +532,7 @@
         tok = args[0].shape[0]
         if tok == LANES and takes_fused(shape, w_down.shape[2], w_down.shape[1], capacity):
             return tuple(
-                v[None] if i == 2 else v for i, v in enumerate(fused_shards(shape["dp"], *args))
+                v[None] if i == 2 else v.T if i == 1 else v for i, v in enumerate(fused_shards(shape["dp"], *args))
             )
         return shards(*args)
 

time: 77 us -> 75.1 us (0.975)
  other arithmetic: 1.35 us -> 0 us
  local copies, waits for them, and re-layouts: 6.06 us -> 5.09 us
    convert_element_type x2 -> x0, other arithmetic: 1.34 us -> none  [the longest x1 0.68 us: fused_shards(): route_ids.astype(F32)]
where the time goes in v3:
time: 75.1 us; the launch traced here: 74.6 us
  Pallas kernels  68.9 us (92%)
  local copies, waits for them, and re-layouts  5.09 us (7%)
    pallas_call x1, Pallas kernels, fused_shards(): pl.pallas_call(functools.partial(fused, n_z, cap, nb), out_shape=(jax.Sha...  68.9 us
    unnamed x3, local copies, waits for them, and re-layouts  5.09 us

profile of v3, /device:TPU:0, one launch (start us, length us, event | category | flops | bytes accessed | tf_op | source)
XLA Modules:
  0.0 74.6 jit_solution(15714480725658759095)
XLA Ops:
  0.6 68.9 %shard_map.94 = (bf16[128,2048]{1,0:T(8,128)(2,1)}, bf16[2,128]{1,0:T(2,128)(2,1)}, bf16[192,2048]{1,0:T(8,128)(2,1)}) custom-call(s32[2,128]{1,0:T(2,128)} %bitcast.13, bf16[2,128]{1,0:T(2,128)(2,1)} %bitcast.14, bf16[128,2048]{1,0:T(8,128)(2,1)} %tok_hbm.1, bf16[320,1536]{1,0:T(8,128)(2,1)} %bitcast.11, bf16[2048,768]{1,0:T(8,128)(2,1)} %bitcast.8, ...), custom_call_target="tpu_custom_call" | custom-call | tf_op jit(solution)/shard_map/pallas_call | solution.py:381
  69.5 1.9 %copy.13 = bf16[128,2048]{1,0:T(8,128)(2,1)} copy(bf16[128,2048]{1,0:T(8,128)(2,1)} %get-tuple-element.12) | data formatting | bytes 1048576
  71.4 1.1 %copy.14 = bf16[128,2]{0,1:T(2,128)(2,1)} copy(bf16[128,2]{0,1:T(2,128)(2,1)} %bitcast.15) | data formatting | bytes 1024
  72.5 2.1 %copy.15 = bf16[1,192,2048]{2,1,0:T(8,128)(2,1)} copy(bf16[1,192,2048]{2,1,0:T(8,128)(2,1)} %bitcast.12) | data formatting | bytes 1572864

commit v4 on v3

--- a/solution.py
+++ b/solution.py
@@ -10,7 +10,7 @@
 MESH = pl.DeviceIdType.MESH
 BF16, F32 = jnp.bfloat16, jnp.float32
 LANES = 128
-BLOCKS = 8
+BLOCKS = 4
 
 
 def dot(a, b, ca=1, cb=0):

time: 75.1 us -> 74.4 us (level)
  no operation moved by 1% of the time
where the time goes in v4:
time: 74.4 us; the launch traced here: 74.2 us
  Pallas kernels  68.5 us (92%)
  local copies, waits for them, and re-layouts  5.09 us (7%)
    pallas_call x1, Pallas kernels, fused_shards(): pl.pallas_call(functools.partial(fused, n_z, cap, nb), out_shape=(jax.Sha...  68.5 us
    unnamed x3, local copies, waits for them, and re-layouts  5.09 us

profile of v4, /device:TPU:0, one launch (start us, length us, event | category | flops | bytes accessed | tf_op | source)
XLA Modules:
  0.0 74.2 jit_solution(12660248760434912224)
XLA Ops:
  0.6 68.5 %shard_map.94 = (bf16[128,2048]{1,0:T(8,128)(2,1)}, bf16[2,128]{1,0:T(2,128)(2,1)}, bf16[192,2048]{1,0:T(8,128)(2,1)}) custom-call(s32[2,128]{1,0:T(2,128)} %bitcast.13, bf16[2,128]{1,0:T(2,128)(2,1)} %bitcast.14, bf16[128,2048]{1,0:T(8,128)(2,1)} %tok_hbm.1, bf16[320,1536]{1,0:T(8,128)(2,1)} %bitcast.11, bf16[2048,768]{1,0:T(8,128)(2,1)} %bitcast.8, ...), custom_call_target="tpu_custom_call" | custom-call | tf_op jit(solution)/shard_map/pallas_call | solution.py:381
  69.1 1.9 %copy.13 = bf16[128,2048]{1,0:T(8,128)(2,1)} copy(bf16[128,2048]{1,0:T(8,128)(2,1)} %get-tuple-element.12) | data formatting | bytes 1048576
  71.0 1.1 %copy.14 = bf16[128,2]{0,1:T(2,128)(2,1)} copy(bf16[128,2]{0,1:T(2,128)(2,1)} %bitcast.15) | data formatting | bytes 1024
  72.1 2.1 %copy.15 = bf16[1,192,2048]{2,1,0:T(8,128)(2,1)} copy(bf16[1,192,2048]{2,1,0:T(8,128)(2,1)} %bitcast.12) | data formatting | bytes 1572864
